TPU v7x, 128 devices: a whole 4x4x4 slice. The times are simulated.
128 devices in a mesh: clu: 16 (over x, z), tile: 8 (over y, core).
Axes of the slice: x: 4, y: 4, z: 4, core: 2. Of those that a mesh axis runs over, the one named last changes fastest.
Arguments:
- embeddings: bfloat16 [163840, 768], P(('clu', 'tile')), may hold values from -32 to 32
- cluster: int32 [163840], P(('clu', 'tile')), may hold values from 0 to 127, as said below
- owner_map: int32 [128], replicated, may hold values from 0 to 15, as said below
Outputs:
- best_match: float32 [163840], P(('clu', 'tile'))
Inputs may be any that keep to these rules, and one draw needn't show every extreme that they name: `cluster`: among the 1280 rows of each device (aligned blocks of 1280 rows), the clusters owned by each owner (through owner_map) are named exactly 1280 / 16 times. `owner_map`: each owner index is named by exactly 8 clusters.
All inputs are finite; a program needn't handle non-finite values.
Results may differ from a plain program's by a relative error of at most 0.00077.
Values may be sent and summed in bfloat16 or wider, within the bound.
A program may use at most 192 MiB of HBM per device.

v0:
```python
import jax
import jax.numpy as jnp
from jax import lax
from jax.sharding import PartitionSpec as P


def compare_rows(best, mine, piece):
    my_unit, my_clu, my_glob = mine
    cand_unit, cand_clu, cand_glob = piece
    count = cand_unit.shape[0]
    width = my_unit.shape[0]

    def one_block(running, block_items):
        b_unit, b_clu, b_glob = block_items
        scores = lax.dot_general(
            my_unit, b_unit, (((1,), (1,)), ((), ())), preferred_element_type=jnp.float32
        )
        allowed = (my_clu[:, None] == b_clu[None, :]) & (my_glob[:, None] > b_glob[None, :])
        return (
            jnp.maximum(running, jnp.max(jnp.where(allowed, scores, jnp.float32(-1.0)), axis=1)),
            None,
        )

    blocks = (
        cand_unit.reshape(count // width, width, cand_unit.shape[1]),
        cand_clu.reshape(count // width, width),
        cand_glob.reshape(count // width, width),
    )
    best, unused = lax.scan(one_block, best, blocks)
    return best


def on_device(embeddings, cluster, owner_map):
    rows = embeddings.shape[0]
    width = embeddings.shape[1]
    n_clu = lax.axis_size("clu")
    n_tile = lax.axis_size("tile")
    share = rows // n_clu
    values = embeddings.astype(jnp.float32)
    unit = (values * lax.rsqrt(jnp.sum(values * values, axis=1, keepdims=True) + 1e-06)).astype(
        jnp.bfloat16
    )
    labels = lax.iota(jnp.int32, owner_map.shape[0])
    owner = jnp.sum(jnp.where(cluster[:, None] == labels[None, :], owner_map[None, :], 0), axis=1)
    order = jnp.argsort(owner, stable=True)
    base = (lax.axis_index("clu") * n_tile + lax.axis_index("tile")) * rows
    position = base + lax.iota(jnp.int32, rows)
    sorted_unit = unit[order].reshape(n_clu, share, width)
    sorted_clu = cluster[order].reshape(n_clu, share)
    sorted_pos = position[order].reshape(n_clu, share)
    empty = jnp.full((rows,), -1.0, jnp.float32)
    tile_unit, tile_clu, tile_pos = (
        lax.all_gather(sorted_unit[None], "tile", axis=0, tiled=True),
        lax.all_gather(sorted_clu[None], "tile", axis=0, tiled=True),
        lax.all_gather(sorted_pos[None], "tile", axis=0, tiled=True),
    )
    group_unit, group_clu, group_pos = (
        lax.all_to_all(tile_unit, "clu", split_axis=1, concat_axis=1, tiled=True),
        lax.all_to_all(tile_clu, "clu", split_axis=1, concat_axis=1, tiled=True),
        lax.all_to_all(tile_pos, "clu", split_axis=1, concat_axis=1, tiled=True),
    )
    here = lax.axis_index("tile")
    mine = (
        lax.dynamic_index_in_dim(group_unit, here, 0, keepdims=False).reshape(rows, width),
        lax.dynamic_index_in_dim(group_clu, here, 0, keepdims=False).reshape(rows),
        lax.dynamic_index_in_dim(group_pos, here, 0, keepdims=False).reshape(rows),
    )
    total = n_tile * rows
    everyone = (
        group_unit.reshape(total, width),
        group_clu.reshape(total),
        group_pos.reshape(total),
    )
    best = compare_rows(empty, mine, everyone)
    returned = lax.all_to_all(
        best.reshape(n_clu, share), "clu", split_axis=0, concat_axis=0, tiled=True
    ).reshape(rows)
    return jnp.zeros((rows,), jnp.float32).at[order].set(returned)


def solution(mesh):
    placed = (P(("clu", "tile"), None), P(("clu", "tile")), P())
    return jax.shard_map(
        on_device, mesh=mesh, in_specs=placed, out_specs=P(("clu", "tile")), check_vma=False
    )
```

profile of v0, /device:TPU:1, one launch (start us, length us, event | category | flops | bytes accessed | tf_op | source)
XLA Modules:
  0.0 482.6 jit_solution(12698412484297944933)
XLA Ops:
  6.5 1.1 select_reduce_fusion
  7.7 5.0 %sort.17 = (s32[1280]{0:T(1024)}, s32[1280]{0:T(1024)S(1)}) sort(s32[1280]{0:T(1024)S(1)} %select_reduce_fusion, s32[1280]{0:T(1024)S(1)} %iota.11), dimensions={0}, to_apply=%region_1.2 | sort | flops 14080 | bytes 20480 | tf_op jit(solution)/shard_map/jit(argsort)/sort | solution.py:45
  12.7 2.1 fusion.7
  15.3 4.9 %gather_fusion.2 = bf16[1280,768]{1,0:T(8,128)(2,1)} fusion(bf16[1280,768]{1,0:T(8,128)(2,1)S(1)} %fusion.8, s32[2048]{0:T(1024)S(1)} %pad_clamp_fusion), kind=kCustom, calls=%fused_computation.2 | custom fusion | bytes 3937280 | tf_op jit(solution)/shard_map/gather | solution.py:48
  20.3 0.7 copy-done
  20.9 7.1 %gather_fusion = s32[1280]{0:T(1024)S(1)} fusion(s32[1280]{0:T(1024)S(1)} %copy-done, s32[2048]{0:T(1024)S(1)} %pad_clamp_fusion), kind=kCustom, calls=%fused_computation | custom fusion | bytes 15360 | tf_op jit(solution)/shard_map/gather | solution.py:49
  28.1 14.6 %all_gather.9 = s32[8,16,80]{2,1,0:T(8,128)S(1)} all-gather(s32[1,16,80]{2,1,0:T(8,128)S(1)} %broadcast_in_dim_reshape.11), channel_id=1, replica_groups=mesh['clu'=16,'tile'=8] {'tile'}, dimensions={0}, use_global_device_ids=true | all-gather | bytes 46080 | tf_op jit(solution)/shard_map/all_gather | solution.py:54
  42.7 0.6 copy.13
  43.3 7.6 %all-to-all-start = ((s32[8,16,80]{2,0,1:T(8,128)}), s32[8,16,80]{2,0,1:T(8,128)S(1)}, u32[]{:S(2)}, u32[]{:S(2)}) async-start(s32[8,16,80]{2,0,1:T(8,128)} %copy.13), calls=%async_computation | async-start | bytes 131072 | tf_op jit(solution)/shard_map/all_to_all | solution.py:59
  50.9 7.1 %gather_fusion.1 = s32[1280]{0:T(1024)S(1)} fusion(s32[1280]{0:T(1024)S(1)} %iota_add_fusion, s32[2048]{0:T(1024)S(1)} %pad_clamp_fusion), kind=kCustom, calls=%fused_computation.1 | custom fusion | bytes 15360 | tf_op jit(solution)/shard_map/gather | solution.py:50
  58.1 13.1 %all_gather.10 = s32[8,16,80]{2,1,0:T(8,128)S(1)} all-gather(s32[1,16,80]{2,1,0:T(8,128)S(1)} %broadcast_in_dim_reshape.12), channel_id=1, replica_groups=mesh['clu'=16,'tile'=8] {'tile'}, dimensions={0}, use_global_device_ids=true | all-gather | bytes 46080 | tf_op jit(solution)/shard_map/all_gather | solution.py:55
  71.2 0.6 copy.15
  71.8 6.9 %all-to-all-start.1 = ((s32[8,16,80]{2,0,1:T(8,128)}), s32[8,16,80]{2,0,1:T(8,128)S(1)}, u32[]{:S(2)}, u32[]{:S(2)}) async-start(s32[8,16,80]{2,0,1:T(8,128)} %copy.15), calls=%async_computation.1 | async-start | bytes 131072 | tf_op jit(solution)/shard_map/all_to_all | solution.py:60
  78.8 26.3 %all-gather.2.cloned.1.call-done = bf16[8,16,80,768]{3,2,1,0:T(8,128)(2,1)} async-done(((bf16[1,16,80,768]{3,2,1,0:T(8,128)(2,1)}), bf16[8,16,80,768]{3,2,1,0:T(8,128)(2,1)}) %all-gather.2.cloned.1.call-update) | async-done | bytes 15728656 | tf_op jit(solution)/shard_map/all_gather | solution.py:53
  105.0 13.3 %copy.17 = bf16[8,16,80,768]{3,2,0,1:T(8,128)(2,1)} copy(bf16[8,16,80,768]{3,2,1,0:T(8,128)(2,1)} %all-gather.2.cloned.1.call-done) | data formatting | bytes 31457280 | tf_op jit(solution)/shard_map/all_gather | solution.py:53
  118.3 6.7 %all-to-all-start.2 = ((bf16[8,16,80,768]{3,2,0,1:T(8,128)(2,1)}), bf16[8,16,80,768]{3,2,0,1:T(8,128)(2,1)}, u32[]{:S(2)}, u32[]{:S(2)}) async-start(bf16[8,16,80,768]{3,2,0,1:T(8,128)(2,1)} %copy.17), calls=%async_computation.2 | async-start | bytes 31457280 | tf_op jit(solution)/shard_map/all_to_all | solution.py:58
  125.5 276.1 %all-to-all-done.2 = bf16[8,16,80,768]{3,2,0,1:T(8,128)(2,1)} async-done(((bf16[8,16,80,768]{3,2,0,1:T(8,128)(2,1)}), bf16[8,16,80,768]{3,2,0,1:T(8,128)(2,1)}, u32[]{:S(2)}, u32[]{:S(2)}) %all-to-all-start.2) | async-done | bytes 15728672 | tf_op jit(solution)/shard_map/all_to_all | solution.py:58
  401.6 13.2 %copy.18 = bf16[8,16,80,768]{3,2,1,0:T(8,128)(2,1)} copy(bf16[8,16,80,768]{3,2,0,1:T(8,128)(2,1)} %all-to-all-done.2) | data formatting | bytes 31457280 | tf_op jit(solution)/shard_map/all_to_all | solution.py:58
  414.8 1.7 constant_dynamic-slice_fusion
  416.5 36.7 %while.12 = (s32[]{:T(128)}, f32[1280]{0:T(1024)S(1)}, s32[16,80]{1,0:T(8,128)}, s32[8,1280]{1,0:T(8,128)S(1)}, s32[16,80]{1,0:T(8,128)}, /*index=5*/s32[8,1280]...) while((s32[]{:T(128)}, f32[1280]{0:T(1024)S(1)}, ...), condition=%wide.wide.region_5.6_spmd.clone, body=%wide.wide.region_3.5_spmd.clone.sunk | while | flops 2524775680 | bytes 3993743 | solution.py:29
  416.6 4.5 fusion.20
  421.2 4.5 fusion.20
  425.8 4.5 fusion.20
  430.3 4.5 fusion.20
  434.9 4.5 fusion.20
  439.5 4.5 fusion.20
  444.1 4.5 fusion.20
  448.7 4.5 fusion.20
  453.3 15.3 %all_to_all.24 = f32[16,1,80]{2,1,0:T(1,128)S(1)} all-to-all(f32[16,1,80]{2,1,0:T(1,128)S(1)} %all_to_all.18), channel_id=1, replica_groups=mesh['clu'=16,'tile'=8] {'clu'}, dimensions={0} | all-to-all | bytes 10240 | tf_op jit(solution)/shard_map/all_to_all | solution.py:75
  468.7 0.5 broadcast.36
  469.2 0.7 reduce.7
  469.9 5.8 %scatter_custom_fusion = f32[1280]{0:T(1024)} fusion(s32[1280]{0:T(1024)S(1)} %compare_select_fusion, f32[1280]{0:T(1024)S(1)} %reshape.52, f32[]{:T(128)} %constant.21.clone.1), kind=kCustom, calls=%fused_computation.23 | custom fusion | bytes 5124 | tf_op jit(solution)/shard_map/scatter | solution.py:78
  (46 shorter events, 1.5 us)
Async XLA Ops:
  6.5 98.5 %all-gather.2.cloned.1.call-start = ((), (), s32[]{:S(2)}) async-start(), calls=%async_computation.4 | async-start | bytes 17694720 | tf_op jit(solution)/shard_map/all_gather | solution.py:53
  12.7 2.2 copy-start.1
  20.2 0.7 copy-start
  43.3 28.5 %all-to-all-start = ((s32[8,16,80]{2,0,1:T(8,128)}), s32[8,16,80]{2,0,1:T(8,128)S(1)}, u32[]{:S(2)}, u32[]{:S(2)}) async-start(s32[8,16,80]{2,0,1:T(8,128)} %copy.13), calls=%async_computation | async-start | bytes 131072 | tf_op jit(solution)/shard_map/all_to_all | solution.py:59
  71.8 46.5 %all-to-all-start.1 = ((s32[8,16,80]{2,0,1:T(8,128)}), s32[8,16,80]{2,0,1:T(8,128)S(1)}, u32[]{:S(2)}, u32[]{:S(2)}) async-start(s32[8,16,80]{2,0,1:T(8,128)} %copy.15), calls=%async_computation.1 | async-start | bytes 131072 | tf_op jit(solution)/shard_map/all_to_all | solution.py:60
  118.3 283.3 %all-to-all-start.2 = ((bf16[8,16,80,768]{3,2,0,1:T(8,128)(2,1)}), bf16[8,16,80,768]{3,2,0,1:T(8,128)(2,1)}, u32[]{:S(2)}, u32[]{:S(2)}) async-start(bf16[8,16,80,768]{3,2,0,1:T(8,128)(2,1)} %copy.17), calls=%async_computation.2 | async-start | bytes 31457280 | tf_op jit(solution)/shard_map/all_to_all | solution.py:58
  125.3 289.6 %copy-start.2 = (s32[1,16,80]{2,0,1:T(1,128)}, s32[1,16,80]{2,0,1:T(1,128)S(1)}, u32[]{:S(2)}) copy-start(s32[1,16,80]{2,0,1:T(1,128)S(1)} %constant_dynamic-slice_fusion.1) | copy-start | bytes 15364
  125.4 289.5 %copy-start.3 = (s32[1,16,80]{2,0,1:T(1,128)}, s32[1,16,80]{2,0,1:T(1,128)S(1)}, u32[]{:S(2)}) copy-start(s32[1,16,80]{2,0,1:T(1,128)S(1)} %constant_dynamic-slice_fusion.2) | copy-start | bytes 15364
Sparse Core Ops, SparseCore 0:
  20.4 84.5 all-gather.1
where the time goes:
time: 485 us; the launch traced here: 483 us
  waiting for transfers between devices  302 us (62%)
  local copies, waits for them, and re-layouts  56.6 us (12%)
  blocking collectives  43 us (9%)
  matrix products  36 us (7%)
  starting transfers between devices  21.2 us (4%)
  between operations  13.6 us (3%)
  other arithmetic  9.45 us (2%)
    all_to_all x1, waiting for transfers between devices, on_device(): lax.all_to_all(tile_unit, 'clu', split_axis=1, concat_axis=1, tiled=True)  276 us
    dot_general x8, matrix products, one_block(): lax.dot_general(my_unit, b_unit, (((1,), (1,)), ((), ())), preferred_elem...  36 us
    all_gather x1, waiting for transfers between devices, on_device(): lax.all_gather(sorted_unit[None], 'tile', axis=0, tiled=True)  26.3 us
    all_to_all x1, blocking collectives, on_device(): lax.all_to_all(best.reshape(n_clu, share), 'clu', split_axis=0, concat_ax...  15.3 us
    all_gather x1, blocking collectives, on_device(): lax.all_gather(sorted_clu[None], 'tile', axis=0, tiled=True)  14.6 us
    all_gather x1, local copies, waits for them, and re-layouts, on_device(): lax.all_gather(sorted_unit[None], 'tile', axis=0, tiled=True)  13.3 us
    all_to_all x1, local copies, waits for them, and re-layouts, on_device(): lax.all_to_all(tile_unit, 'clu', split_axis=1, concat_axis=1, tiled=True)  13.2 us
    all_gather x1, blocking collectives, on_device(): lax.all_gather(sorted_pos[None], 'tile', axis=0, tiled=True)  13.1 us
  transfers between devices with their start and end apart: 4, of which 2 were waited for; matrix products, arithmetic and copies ran while one was open for 6% of the time, Pallas kernels for 0%

commit v1 on v0

v1 whole, which is shorter than its diff:
```python
import functools

import jax
import jax.numpy as jnp
from jax import lax
from jax.experimental import pallas as pl
from jax.experimental.pallas import tpu as pltpu
from jax.sharding import PartitionSpec as P

MESH = pl.DeviceIdType.MESH
F32 = jnp.float32
BF16 = jnp.bfloat16

SIDE = 4
OFFS = [(dx, dz) for dx in range(SIDE) for dz in range(SIDE)]
N_OWN = len(OFFS)
ROWS = 1280
SHARE = ROWS // N_OWN
WIDTH = 768
STAGES = [4, 4, 4, 4]

PAIRS = [(0, 0), (0, 1), (0, 3), (0, 2), (1, 3), (1, 2), (2, 3), (2, 4)]


def dot_t(a, b):
    return lax.dot_general(a, b, (((1,), (1,)), ((), ())), preferred_element_type=F32)


def dot(a, b):
    return jnp.dot(a, b, preferred_element_type=F32)


def split3(v):
    hi = v.astype(BF16)
    rest = v - hi.astype(F32)
    mid = rest.astype(BF16)
    low = (rest - mid.astype(F32)).astype(BF16)
    return jnp.concatenate([hi, mid, low], axis=0)


def iota(shape, dim):
    return lax.broadcasted_iota(jnp.int32, shape, dim)


def onehot(mask):
    return jnp.where(mask, F32(1.0), F32(0.0)).astype(BF16)


def kernel(
    emb, clu, omap, out,
    unit, outbox, held, msend, meta, onehot_rank, own_mask,
    lane_clu, col_info, rowacc, colacc, resend, reget, retsend, retget,
    a_s, a_r, m_s, m_r, f_s, f_r, g_s, g_r, s_s, s_r, q_s, q_r, t_s, t_r,
):
    c = lax.axis_index("clu")
    t = lax.axis_index("tile")
    x, z, y, k = c // SIDE, c % SIDE, t // 2, t % 2

    def shifted(dx, dz):
        return ((x + dx) % SIDE) * SIDE + (z + dz) % SIDE

    dest = [shifted(dx, dz) for dx, dz in OFFS]
    origin = [shifted(SIDE - dx, SIDE - dz) for dx, dz in OFFS]
    up, down = (y + 1) % SIDE, (y + SIDE - 1) % SIDE
    sib = (c, 2 * y + (1 - k))
    above, below = (c, 2 * up + k), (c, 2 * down + k)
    above_x, below_x = (c, 2 * up + (1 - k)), (c, 2 * down + (1 - k))

    barrier = pltpu.get_barrier_semaphore()
    peers = [(d, t) for d in dest[1:]] + [sib, above, below, above_x, below_x]
    for peer in peers:
        pl.semaphore_signal(barrier, inc=1, device_id=peer, device_id_type=MESH)

    def copy(src, dst, ssem, rsem, device):
        return pltpu.make_async_remote_copy(
            src_ref=src, dst_ref=dst, send_sem=ssem, recv_sem=rsem,
            device_id=device, device_id_type=MESH,
        )

    def block(j, n=1):
        return pl.ds(j * SHARE, n * SHARE)

    def normalise(i, carry):
        rows = pl.ds(i * SHARE, SHARE)
        v = emb[rows, :].astype(F32)
        unit[rows, :] = (v * lax.rsqrt(jnp.sum(v * v, axis=1, keepdims=True) + 1e-06)).astype(BF16)
        return carry

    lax.fori_loop(0, N_OWN, normalise, 0)

    ids = clu[...]
    which = onehot(iota((omap.shape[1], ROWS), 0) == ids)
    step = iota((N_OWN, omap.shape[1]), 0)
    owner_of = jnp.zeros((N_OWN, omap.shape[1]), jnp.int32)
    for j in range(N_OWN):
        owner_of = jnp.where(step == j, dest[j], owner_of)
    mine = dot(onehot(owner_of == omap[...]), which)
    own_mask[...] = mine
    part = 256
    before = onehot(iota((part, part), 0) < iota((part, part), 1))
    base = jnp.zeros((N_OWN, 1), F32)
    pieces = []
    for i in range(ROWS // part):
        piece = mine[:, i * part:(i + 1) * part]
        pieces.append(dot(piece.astype(BF16), before) + base)
        base = base + jnp.sum(piece, axis=1, keepdims=True)
    rank = jnp.sum(mine * jnp.concatenate(pieces, axis=1), axis=0, keepdims=True)
    slot = jnp.sum(mine * iota((N_OWN, ROWS), 0).astype(F32), axis=0, keepdims=True) * SHARE + rank
    slot = slot.astype(jnp.int32)
    at_rank = onehot(iota((128, ROWS), 0) == rank.astype(jnp.int32))
    onehot_rank[...] = at_rank
    labels = dot_t((mine * ids.astype(F32)).astype(BF16), at_rank)
    for j in range(N_OWN):
        msend[j] = jnp.broadcast_to(labels[j:j + 1, :], (8, 128))
    meta[0, 0] = msend[0]

    pl.semaphore_wait(barrier, len(peers))

    meta_out = []
    for j in range(1, N_OWN):
        meta_out.append(copy(msend.at[j], meta.at[0, j], m_s.at[j], m_r.at[j], (dest[j], t)))
        meta_out[-1].start()

    def forward(j):
        n = pl.ds(j * SHARE, SHARE)
        return [
            copy(held.at[0, n], held.at[b, n], f_s.at[b, j], f_r.at[b, j], device)
            for b, device in ((2, above), (3, below), (1, sib))
        ]

    forwards = []
    out_copies = []
    first = 0
    for n in STAGES:
        size = n * SHARE
        take = onehot(iota((size, ROWS), 0) + first * SHARE == slot)
        outbox[block(first, n), :] = dot(take, unit[...]).astype(BF16)
        for j in range(first, first + n):
            if j == 0:
                held[0, block(0), :] = outbox[block(0), :]
                forwards.append(forward(0))
                for cp in forwards[0]:
                    cp.start()
            else:
                cp = copy(
                    outbox.at[block(j)], held.at[0, block(j)], a_s.at[j], a_r.at[j], (dest[j], t)
                )
                cp.start()
                out_copies.append(cp)
        first += n

    position = iota((1, ROWS), 1)
    lane_j = position // SHARE
    lane_k = position - lane_j * SHARE
    lane_key = lane_k
    for j in range(N_OWN):
        lane_key = lane_key + jnp.where(lane_j == j, origin[j] * 1024, 0)
    lane_key = lane_key.astype(F32)
    tile_of = [t, 2 * y + (1 - k), 2 * down + k, 2 * up + k, 2 * up + (1 - k)]
    spread = onehot(iota((128, ROWS), 0) == lane_k)
    in_block = onehot(iota((N_OWN, ROWS), 0) == lane_j).astype(F32)

    for b in range(3):
        rowacc[b] = jnp.full((ROWS, 128), -1.0, F32)
    for b in range(5):
        colacc[b] = jnp.full((1, ROWS), -1.0, F32)

    def wait_own(j):
        out_copies[j - 1].wait_recv()
        forwards.append(forward(j))
        for cp in forwards[j]:
            cp.start()

    for cp in meta_out:
        cp.wait()
    meta_fwd = [
        copy(meta.at[0], meta.at[b], g_s.at[b], g_r.at[b], device)
        for b, device in ((1, sib), (2, above), (3, below), (4, below_x))
    ]
    for cp in meta_fwd:
        cp.start()

    for j in range(1, STAGES[0]):
        wait_own(j)

    for cp in meta_fwd:
        cp.wait()
    for b in range(5):
        lane = jnp.sum(in_block * dot(meta[b, :, 0, :].astype(BF16), spread), axis=0, keepdims=True)
        lane_clu[b] = lane
        if b < 3:
            key = lane_key + (tile_of[b] * 128).astype(F32)
            both = jnp.where(iota((128, ROWS), 0) == 0, lane, key)
            col_info[b] = both.T

    second = []

    def stage(first, n):
        new = block(first, n)
        size = n * SHARE
        seen = (first + n) * SHARE
        for j in range(first, first + n):
            for cp in forwards[j]:
                cp.wait_recv()
            cp = copy(
                held.at[3, block(j)], held.at[4, block(j)], s_s.at[j], s_r.at[j], sib
            )
            cp.start()
            second.append(cp)
        for a, b in PAIRS:
            if b == 4:
                for j in range(first, first + n):
                    second[j].wait_recv()
            scores = dot_t(held[a, new, :], held[b, :seen, :])
            row_clu = col_info[a, new, 0:1]
            row_key = col_info[a, new, 1:2]
            col_clu = lane_clu[b, :, :seen]
            col_key = lane_key[:, :seen] + (tile_of[b] * 128).astype(F32)
            same = jnp.where(row_clu == col_clu, scores, F32(-1.0))
            as_row = jnp.where(row_key > col_key, same, F32(-1.0))
            as_col = jnp.where(row_key < col_key, same, F32(-1.0))
            rowacc[a, new, 0:1] = jnp.maximum(
                rowacc[a, new, 0:1], jnp.max(as_row, axis=1, keepdims=True)
            )
            colacc[b, :, :seen] = jnp.maximum(
                colacc[b, :, :seen], jnp.max(as_col, axis=0, keepdims=True)
            )

    first = STAGES[0]
    done = 0
    for i in range(len(STAGES)):
        if i + 1 < len(STAGES):
            for j in range(first, first + STAGES[i + 1]):
                wait_own(j)
            first += STAGES[i + 1]
        stage(done, STAGES[i])
        done += STAGES[i]

    lanes = iota((ROWS, 128), 1)
    rows_all = jnp.where(
        lanes == 0, rowacc[0, :, 0:1], jnp.where(lanes == 1, rowacc[1, :, 0:1], rowacc[2, :, 0:1])
    ).T
    for b in range(5):
        best = colacc[b]
        if b < 3:
            best = jnp.maximum(best, rows_all[b:b + 1, :])
        resend[b] = jnp.broadcast_to(best, (8, ROWS))
    back = [
        copy(resend.at[b], reget.at[b - 1], q_s.at[b], q_r.at[b], device)
        for b, device in ((1, sib), (2, below), (3, above), (4, above_x))
    ]
    for cp in back:
        cp.start()
    for cp in back:
        cp.wait_recv()
    total = resend[0]
    for b in range(4):
        total = jnp.maximum(total, reget[b])
    parts = dot_t(split3(in_block * total[0:1, :]), spread)
    parts = parts[:N_OWN] + parts[N_OWN:2 * N_OWN] + parts[2 * N_OWN:]
    for j in range(N_OWN):
        retsend[j] = jnp.broadcast_to(parts[j:j + 1, :], (8, 128))
    retget[0] = retsend[0]
    returns = [
        copy(retsend.at[j], retget.at[j], t_s.at[j], t_r.at[j], (origin[j], t))
        for j in range(1, N_OWN)
    ]
    for cp in returns:
        cp.start()
    for cp in returns:
        cp.wait_recv()
    values = dot(split3(retget[:, 0, :]), onehot_rank[...])
    values = values[:N_OWN] + values[N_OWN:2 * N_OWN] + values[2 * N_OWN:]
    out[...] = jnp.sum(values * own_mask[...], axis=0, keepdims=True)

    for cp in out_copies + second + back + returns:
        cp.wait_send()
    for group in forwards:
        for cp in group:
            cp.wait_send()


def on_device(embeddings, cluster, owner_map):
    dma = pltpu.SemaphoreType.DMA
    scratch = [
        pltpu.VMEM((ROWS, WIDTH), BF16),
        pltpu.VMEM((ROWS, WIDTH), BF16),
        pltpu.VMEM((5, ROWS, WIDTH), BF16),
        pltpu.VMEM((N_OWN, 8, 128), F32),
        pltpu.VMEM((5, N_OWN, 8, 128), F32),
        pltpu.VMEM((128, ROWS), BF16),
        pltpu.VMEM((N_OWN, ROWS), F32),
        pltpu.VMEM((5, 1, ROWS), F32),
        pltpu.VMEM((3, ROWS, 128), F32),
        pltpu.VMEM((3, ROWS, 128), F32),
        pltpu.VMEM((5, 1, ROWS), F32),
        pltpu.VMEM((5, 8, ROWS), F32),
        pltpu.VMEM((4, 8, ROWS), F32),
        pltpu.VMEM((N_OWN, 8, 128), F32),
        pltpu.VMEM((N_OWN, 8, 128), F32),
        dma((N_OWN,)), dma((N_OWN,)),
        dma((N_OWN,)), dma((N_OWN,)),
        dma((4, N_OWN)), dma((4, N_OWN)),
        dma((5,)), dma((5,)),
        dma((N_OWN,)), dma((N_OWN,)),
        dma((5,)), dma((5,)),
        dma((N_OWN,)), dma((N_OWN,)),
    ]
    vmem = pl.BlockSpec(memory_space=pltpu.VMEM)
    best = pl.pallas_call(
        kernel,
        out_shape=jax.ShapeDtypeStruct((1, ROWS), F32),
        in_specs=[vmem, vmem, vmem],
        out_specs=vmem,
        scratch_shapes=scratch,
        compiler_params=pltpu.CompilerParams(
            collective_id=0, has_side_effects=True, vmem_limit_bytes=56 << 20
        ),
    )(embeddings, cluster.reshape(1, -1), owner_map.reshape(1, -1))
    return best.reshape(-1)


def solution(mesh):
    placed = (P(("clu", "tile"), None), P(("clu", "tile")), P())
    return jax.shard_map(
        on_device, mesh=mesh, in_specs=placed, out_specs=P(("clu", "tile")), check_vma=False
    )
```

time: 485 us -> 88.4 us (0.18)
  waiting for transfers between devices: 302 us -> 0 us
  Pallas kernels: 0 us -> 85.6 us
  local copies, waits for them, and re-layouts: 56.6 us -> 1.29 us
  blocking collectives: 43 us -> 0 us
  matrix products: 36 us -> 0 us
  starting transfers between devices: 21.2 us -> 0 us
  between operations: 13.6 us -> 0.01 us
  other arithmetic: 9.45 us -> 1.31 us
    all_to_all x3 -> x0, waiting for transfers between devices: 276 us -> none  [the longest x1 276 us: on_device(): lax.all_to_all(tile_unit, 'clu', split_axis=1, concat_axis=1, tiled=True)]
    pallas_call x0 -> x1, Pallas kernels: none -> 85.6 us  [on_device(): pl.pallas_call(kernel, out_shape=jax.ShapeDtypeStruct((1, ROWS), F32), in...]
    dot_general x8 -> x0, matrix products: 36 us -> none  [one_block(): lax.dot_general(my_unit, b_unit, (((1,), (1,)), ((), ())), preferred_elem...]
    all_gather x2 -> x0, blocking collectives: 27.6 us -> none  [the longest x1 14.6 us: on_device(): lax.all_gather(sorted_clu[None], 'tile', axis=0, tiled=True)]
    all_gather x1 -> x0, waiting for transfers between devices: 26.3 us -> none  [on_device(): lax.all_gather(sorted_unit[None], 'tile', axis=0, tiled=True)]
    all_to_all x3 -> x0, starting transfers between devices: 21.2 us -> none  [the longest x1 7.61 us: on_device(): lax.all_to_all(tile_clu, 'clu', split_axis=1, concat_axis=1, tiled=True)]
    gather x3 -> x0, local copies, waits for them, and re-layouts: 19.1 us -> none  [the longest x1 7.08 us: on_device(): sorted_pos = position[order].reshape(n_clu, share)]
    all_to_all x1 -> x0, blocking collectives: 15.3 us -> none  [on_device(): lax.all_to_all(best.reshape(n_clu, share), 'clu', split_axis=0, concat_ax...]
  transfers between devices with their start and end apart: 4 -> 0, of which waited for: 2 -> 0; matrix products, arithmetic and copies ran while one was open for 6% -> 0% of each run, Pallas kernels for 0% -> 0%
where the time goes in v1:
time: 88.4 us; the launch traced here: 88.2 us
  Pallas kernels  85.6 us (97%)
  other arithmetic  1.31 us (1%)
  local copies, waits for them, and re-layouts  1.29 us (1%)
    pallas_call x1, Pallas kernels, on_device(): pl.pallas_call(kernel, out_shape=jax.ShapeDtypeStruct((1, ROWS), F32), in...  85.6 us

profile of v1, /device:TPU:1, one launch (start us, length us, event | category | flops | bytes accessed | tf_op | source)
XLA Modules:
  0.0 88.2 jit_solution(3635139127684183556)
XLA Ops:
  0.0 1.3 %reshape.9.clu = s32[1,1280]{1,0:T(1,128)} reshape(s32[1280]{0:T(1024)} %param.4) | data formatting | bytes 10240 | tf_op jit(solution)/shard_map/reshape | solution.py:319
  1.3 85.6 %shard_map.37 = f32[1,1280]{1,0:T(1,128)} custom-call(bf16[1280,768]{1,0:T(8,128)(2,1)} %emb.1, s32[1,1280]{1,0:T(1,128)} %reshape.9.clu, s32[1,128]{1,0:T(1,128)} %bitcast.1), custom_call_target="tpu_custom_call" | custom-call | tf_op jit(solution)/shard_map/pallas_call | solution.py:310
  86.9 1.3 %reduce = f32[1280]{0:T(1024)} reduce(f32[1,1280]{1,0:T(1,128)} %shard_map.37, f32[]{:T(128)} %constant), dimensions={0}, to_apply=%pallas_call.3.reduce_sub_computation | reduce | bytes 10244 | tf_op jit(solution)/shard_map/pallas_call | solution.py:310

commit v2 on v1

v2 whole, which is shorter than its diff:
```python
import functools

import jax
import jax.numpy as jnp
from jax import lax
from jax.experimental import pallas as pl
from jax.experimental.pallas import tpu as pltpu
from jax.sharding import PartitionSpec as P

MESH = pl.DeviceIdType.MESH
F32 = jnp.float32
BF16 = jnp.bfloat16

SIDE = 4
OFFS = [
    (0, 0),
    (0, 1), (1, 0), (0, 3), (3, 0),
    (1, 1), (3, 3), (1, 3), (3, 1),
    (0, 2), (2, 0), (1, 2), (2, 1),
    (3, 2), (2, 3), (2, 2),
]
N_OWN = len(OFFS)
ROWS = 1280
SHARE = ROWS // N_OWN
WIDTH = 768
GROUPS = [(0, 5), (5, 9), (9, 13), (13, 16)]
STAGES = [(0, 4), (4, 7), (7, 10), (10, 13), (13, 16)]
STRIP = 352
LAG = 3
ORDER = [
    "P0", "S0", "F0", "P1", "S1", "P2", "L", "W1", "F1", "W2", "F2", "S2", "M", "P3", "W3",
    "F3", "W4", "F4", "S3", "O0", "W5", "F5", "W6", "W7", "F6", "O1", "W8", "F7", "A0", "D0",
    "W9", "F8", "X0", "W10", "W11", "F9", "O2", "W12", "F10", "A1", "D1", "W13", "F11", "X1",
    "W14", "W15", "F12", "O3", "O4", "F13", "A2", "D2", "U0", "F14", "X2", "U1", "U2", "F15",
    "A3", "U3", "D3", "X3", "A4", "U4", "D4", "X4",
]


def align(n, m):
    return -(-n // m) * m


STARTS = [0]
for lo, hi in STAGES:
    STARTS.append(STARTS[-1] + align((hi - lo) * SHARE, 128))
TALL = STARTS[-1]
PLACE = [STARTS[s] + (j - lo) * SHARE for s, (lo, hi) in enumerate(STAGES) for j in range(lo, hi)]


def dot_t(a, b):
    return lax.dot_general(a, b, (((1,), (1,)), ((), ())), preferred_element_type=F32)


def dot(a, b):
    return jnp.dot(a, b, preferred_element_type=F32)


def split3(v):
    hi = v.astype(BF16)
    rest = v - hi.astype(F32)
    mid = rest.astype(BF16)
    low = (rest - mid.astype(F32)).astype(BF16)
    return jnp.concatenate([hi, mid, low], axis=0)


def iota(shape, dim):
    return lax.broadcasted_iota(jnp.int32, shape, dim)


def onehot(mask):
    return jnp.where(mask, F32(1.0), F32(0.0)).astype(BF16)


def kernel(
    emb_hbm, clu, omap, out,
    emb, unit, outbox, held, msend, meta, onehot_rank, own_mask,
    lane_clu, lane_keys, col_info, rowacc, lanebest, resend, reget, retsend, retget,
    a_s, a_r, m_s, m_r, f_s, f_r, g_s, g_r, s_s, s_r, q_s, q_r, t_s, t_r, e_s,
):
    c = lax.axis_index("clu")
    t = lax.axis_index("tile")
    x, z, y, k = c // SIDE, c % SIDE, t // 2, t % 2

    def shifted(dx, dz):
        return ((x + dx) % SIDE) * SIDE + (z + dz) % SIDE

    dest = [shifted(dx, dz) for dx, dz in OFFS]
    origin = [shifted(SIDE - dx, SIDE - dz) for dx, dz in OFFS]
    up, down = (y + 1) % SIDE, (y + SIDE - 1) % SIDE
    sib = (c, 2 * y + (1 - k))
    above, below = (c, 2 * up + k), (c, 2 * down + k)
    above_x, below_x = (c, 2 * up + (1 - k)), (c, 2 * down + (1 - k))

    load = pltpu.make_async_copy(emb_hbm, emb, e_s)
    load.start()
    barrier = pltpu.get_barrier_semaphore()
    peers = [(d, t) for d in dest[1:]] + [sib, above, below, above_x, below_x]
    for peer in peers:
        pl.semaphore_signal(barrier, inc=1, device_id=peer, device_id_type=MESH)

    def copy(src, dst, ssem, rsem, device):
        return pltpu.make_async_remote_copy(
            src_ref=src, dst_ref=dst, send_sem=ssem, recv_sem=rsem,
            device_id=device, device_id_type=MESH,
        )

    def block(j, n=1):
        return pl.ds(j * SHARE, n * SHARE)

    def place(j):
        return pl.ds(PLACE[j], SHARE)

    load.wait()
    def normalise(i, carry):
        rows = pl.ds(i * SHARE, SHARE)
        v = emb[rows, :].astype(F32)
        unit[rows, :] = (v * lax.rsqrt(jnp.sum(v * v, axis=1, keepdims=True) + 1e-06)).astype(BF16)
        return carry

    lax.fori_loop(0, N_OWN, normalise, 0)

    for s, (lo, hi) in enumerate(STAGES):
        full = STARTS[s] + (hi - lo) * SHARE
        if STARTS[s + 1] > full:
            for b in range(5):
                held[b, full:STARTS[s + 1], :] = jnp.zeros((STARTS[s + 1] - full, WIDTH), BF16)

    ids = clu[...].reshape(1, ROWS)
    n_clusters = omap.shape[0]
    which = onehot(iota((n_clusters, ROWS), 0) == ids)
    step = iota((N_OWN, n_clusters), 0)
    owner_of = jnp.zeros((N_OWN, n_clusters), jnp.int32)
    for j in range(N_OWN):
        owner_of = jnp.where(step == j, dest[j], owner_of)
    mine = dot(onehot(owner_of == omap[...].reshape(1, n_clusters)), which)
    own_mask[...] = mine
    part = 256
    before = onehot(iota((part, part), 0) < iota((part, part), 1))
    base = jnp.zeros((N_OWN, 1), F32)
    pieces = []
    for i in range(ROWS // part):
        piece = mine[:, i * part:(i + 1) * part]
        pieces.append(dot(piece.astype(BF16), before) + base)
        base = base + jnp.sum(piece, axis=1, keepdims=True)
    rank = jnp.sum(mine * jnp.concatenate(pieces, axis=1), axis=0, keepdims=True)
    slot = jnp.sum(mine * iota((N_OWN, ROWS), 0).astype(F32), axis=0, keepdims=True) * SHARE + rank
    slot = slot.astype(jnp.int32)
    at_rank = onehot(iota((128, ROWS), 0) == rank.astype(jnp.int32))
    onehot_rank[...] = at_rank
    labels = dot_t((mine * ids.astype(F32)).astype(BF16), at_rank)
    for j in range(N_OWN):
        msend[j] = labels[j:j + 1, :]
    meta[0, 0] = msend[0]

    pl.semaphore_wait(barrier, len(peers))

    meta_out = []
    for j in range(1, N_OWN):
        meta_out.append(copy(msend.at[j], meta.at[0, j], m_s.at[j], m_r.at[j], (dest[j], t)))
        meta_out[-1].start()

    along, across = {}, {}
    out_copies = {}

    def pass_across(j):
        across[j] = copy(held.at[0, place(j)], held.at[1, place(j)], f_s.at[1, j], f_r.at[1, j], sib)
        across[j].start()

    def pass_along(j):
        if j >= LAG:
            for cp in along[j - LAG]:
                cp.wait_send()
        along[j] = [
            copy(held.at[0, place(j)], held.at[b, place(j)], f_s.at[b, j], f_r.at[b, j], device)
            for b, device in ((2, above), (3, below))
        ]
        for cp in along[j]:
            cp.start()

    def prepare(g):
        lo, hi = GROUPS[g]
        take = onehot(iota(((hi - lo) * SHARE, ROWS), 0) + lo * SHARE == slot)
        outbox[block(lo, hi - lo), :] = dot(take, unit[...]).astype(BF16)
        if lo == 0:
            held[0, place(0), :] = outbox[block(0), :]
            pass_across(0)

    def send(g):
        for j in range(max(GROUPS[g][0], 1), GROUPS[g][1]):
            out_copies[j] = copy(
                outbox.at[block(j)], held.at[0, place(j)], a_s.at[j], a_r.at[j], (dest[j], t)
            )
            out_copies[j].start()

    def receive(j):
        out_copies[j].wait_recv()
        pass_across(j)

    position = iota((1, TALL), 1)
    lane_j = jnp.full((1, TALL), -1, jnp.int32)
    lane_k = jnp.full((1, TALL), -1, jnp.int32)
    lane_key = jnp.zeros((1, TALL), jnp.int32)
    for j in range(N_OWN):
        inside = (position >= PLACE[j]) & (position < PLACE[j] + SHARE)
        lane_j = jnp.where(inside, j, lane_j)
        lane_k = jnp.where(inside, position - PLACE[j], lane_k)
        lane_key = jnp.where(inside, origin[j] * 1024 + position - PLACE[j], lane_key)
    lane_key = lane_key.astype(F32)
    tile_of = [t, 2 * y + (1 - k), 2 * down + k, 2 * up + k, 2 * up + (1 - k)]
    spread = onehot(iota((128, TALL), 0) == lane_k)
    in_block = onehot(iota((N_OWN, TALL), 0) == lane_j).astype(F32)

    for b in range(5):
        rowacc[b] = jnp.full((TALL, 128), -1.0, F32)
        lanebest[b] = jnp.full((1, TALL), -1.0, F32)

    meta_fwd = []

    def pass_labels():
        for cp in meta_out:
            cp.wait()
        for b, device in ((1, sib), (2, above), (3, below), (4, below_x)):
            meta_fwd.append(copy(meta.at[0], meta.at[b], g_s.at[b], g_r.at[b], device))
            meta_fwd[-1].start()

    def take_labels():
        for cp in meta_fwd:
            cp.wait()
        for b in range(5):
            lane = jnp.sum(
                in_block * dot(meta[b, :, 0, :].astype(BF16), spread), axis=0, keepdims=True
            )
            lane = jnp.where(lane_j >= 0, lane, F32(-1.0))
            key = lane_key + (tile_of[b] * 128).astype(F32)
            lane_clu[b] = lane
            lane_keys[b] = key
            col_info[b] = jnp.where(iota((128, TALL), 0) == 0, lane, key).T

    second = {}

    def compare(a, b, s, rows):
        width = STARTS[s + 1] - STARTS[s]
        new = pl.ds(STARTS[s], width)
        col_clu = lane_clu[a, :, new]
        col_key = lane_keys[a, :, new]
        best = lanebest[a, :, new]
        for top in range(0, rows, STRIP):
            strip = pl.ds(top, min(STRIP, rows - top))
            scores = dot_t(held[b, strip, :], held[a, new, :])
            same = jnp.where(col_info[b, strip, 0:1] == col_clu, scores, F32(-1.0))
            row_key = col_info[b, strip, 1:2]
            as_row = jnp.where(row_key > col_key, same, F32(-1.0))
            as_col = jnp.where(row_key < col_key, same, F32(-1.0))
            best = jnp.maximum(best, jnp.max(as_col, axis=0, keepdims=True))
            part = rowacc[b, strip, :]
            for i in range(0, width, 128):
                part = jnp.maximum(part, as_row[:, i:i + 128])
            rowacc[b, strip, :] = part
        lanebest[a, :, new] = best

    def inner(s):
        for j in range(*STAGES[s]):
            across[j].wait_recv()
        for b in (0, 1):
            compare(0, b, s, STARTS[s + 1])

    def arrive(s):
        for j in range(*STAGES[s]):
            for cp in along[j]:
                cp.wait_recv()
            second[j] = copy(held.at[3, place(j)], held.at[4, place(j)], s_s.at[j], s_r.at[j], sib)
            second[j].start()

    def with_owners(s):
        compare(3, 0, s, TALL)
        compare(3, 1, s, TALL)

    def with_above(s):
        compare(2, 3, s, STARTS[s + 1])

    def with_far(s):
        for j in range(*STAGES[s]):
            second[j].wait_recv()
        compare(2, 4, s, STARTS[s + 1])

    for action in ORDER:
        what, i = action[0], int(action[1:] or 0)
        if what == "P":
            prepare(i)
        elif what == "S":
            send(i)
        elif what == "W":
            receive(i)
        elif what == "F":
            pass_along(i)
        elif what == "L":
            pass_labels()
        elif what == "M":
            take_labels()
        elif what == "O":
            inner(i)
        elif what == "U":
            with_owners(i)
        elif what == "A":
            arrive(i)
        elif what == "D":
            with_above(i)
        else:
            with_far(i)

    for b in range(5):
        best = lanebest[b]
        if b != 2:
            best = jnp.maximum(best, jnp.max(rowacc[b].T, axis=0, keepdims=True))
        resend[b] = best
    back = [
        copy(resend.at[b], reget.at[b - 1], q_s.at[b], q_r.at[b], device)
        for b, device in ((1, sib), (2, below), (3, above), (4, above_x))
    ]
    for cp in back:
        cp.start()
    for cp in back:
        cp.wait_recv()
    total = resend[0]
    for b in range(4):
        total = jnp.maximum(total, reget[b])
    parts = dot_t(split3(in_block * total), spread)
    parts = parts[:N_OWN] + parts[N_OWN:2 * N_OWN] + parts[2 * N_OWN:]
    for j in range(N_OWN):
        retsend[j] = parts[j:j + 1, :]
    retget[0] = retsend[0]
    returns = [
        copy(retsend.at[j], retget.at[j], t_s.at[j], t_r.at[j], (origin[j], t))
        for j in range(1, N_OWN)
    ]
    for cp in returns:
        cp.start()
    for cp in returns:
        cp.wait_recv()
    values = dot(split3(retget[:, 0, :]), onehot_rank[...])
    values = values[:N_OWN] + values[N_OWN:2 * N_OWN] + values[2 * N_OWN:]
    out[...] = jnp.sum(values * own_mask[...], axis=0)

    left = [cp for j in range(N_OWN - LAG, N_OWN) for cp in along[j]]
    for cp in [*out_copies.values(), *across.values(), *second.values(), *left, *back, *returns]:
        cp.wait_send()


def on_device(embeddings, cluster, owner_map):
    dma = pltpu.SemaphoreType.DMA
    scratch = [
        pltpu.VMEM((ROWS, WIDTH), BF16),
        pltpu.VMEM((ROWS, WIDTH), BF16),
        pltpu.VMEM((ROWS, WIDTH), BF16),
        pltpu.VMEM((5, TALL, WIDTH), BF16),
        pltpu.VMEM((N_OWN, 1, 128), F32),
        pltpu.VMEM((5, N_OWN, 1, 128), F32),
        pltpu.VMEM((128, ROWS), BF16),
        pltpu.VMEM((N_OWN, ROWS), F32),
        pltpu.VMEM((5, 1, TALL), F32),
        pltpu.VMEM((5, 1, TALL), F32),
        pltpu.VMEM((5, TALL, 128), F32),
        pltpu.VMEM((5, TALL, 128), F32),
        pltpu.VMEM((5, 1, TALL), F32),
        pltpu.VMEM((5, 1, TALL), F32),
        pltpu.VMEM((4, 1, TALL), F32),
        pltpu.VMEM((N_OWN, 1, 128), F32),
        pltpu.VMEM((N_OWN, 1, 128), F32),
        dma((N_OWN,)), dma((N_OWN,)),
        dma((N_OWN,)), dma((N_OWN,)),
        dma((4, N_OWN)), dma((4, N_OWN)),
        dma((5,)), dma((5,)),
        dma((N_OWN,)), dma((N_OWN,)),
        dma((5,)), dma((5,)),
        dma((N_OWN,)), dma((N_OWN,)),
        dma,
    ]
    vmem = pl.BlockSpec(memory_space=pltpu.VMEM)
    best = pl.pallas_call(
        kernel,
        out_shape=jax.ShapeDtypeStruct((ROWS,), F32),
        in_specs=[pl.BlockSpec(memory_space=pl.ANY), vmem, vmem],
        out_specs=vmem,
        scratch_shapes=scratch,
        compiler_params=pltpu.CompilerParams(
            collective_id=0, has_side_effects=True, vmem_limit_bytes=56 << 20
        ),
    )(embeddings, cluster, owner_map)
    return best


def solution(mesh):
    placed = (P(("clu", "tile"), None), P(("clu", "tile")), P())
    return jax.shard_map(
        on_device, mesh=mesh, in_specs=placed, out_specs=P(("clu", "tile")), check_vma=False
    )
```

time: 88.4 us -> 73.9 us (0.84)
  Pallas kernels: 85.6 us -> 72.4 us
  other arithmetic: 1.31 us -> 0 us
    pallas_call x1, Pallas kernels: 85.6 us -> 72.4 us  [on_device(): pl.pallas_call(kernel, out_shape=jax.ShapeDtypeStruct((ROWS,), F32), in_s...]
    pallas_call x1 -> x0, other arithmetic: 1.31 us -> none  [on_device(): pl.pallas_call(kernel, out_shape=jax.ShapeDtypeStruct((1, ROWS), F32), in...]
    unnamed x0 -> x1, local copies, waits for them, and re-layouts: none -> 1.3 us
    reshape x1 -> x0, local copies, waits for them, and re-layouts: 1.29 us -> none  [on_device(): cluster.reshape(1, -1)]
where the time goes in v2:
time: 73.9 us; the launch traced here: 73.7 us
  Pallas kernels  72.4 us (98%)
  local copies, waits for them, and re-layouts  1.3 us (2%)
    pallas_call x1, Pallas kernels, on_device(): pl.pallas_call(kernel, out_shape=jax.ShapeDtypeStruct((ROWS,), F32), in_s...  72.4 us

profile of v2, /device:TPU:1, one launch (start us, length us, event | category | flops | bytes accessed | tf_op | source)
XLA Modules:
  0.0 73.7 jit_solution(14335144938922565054)
XLA Ops:
  0.0 72.4 %shard_map.37 = f32[1280]{0:T(1024)} custom-call(bf16[1280,768]{1,0:T(8,128)(2,1)} %emb_hbm.1, s32[1280]{0:T(1024)} %clu.1, s32[128]{0:T(128)} %omap.1), custom_call_target="tpu_custom_call" | custom-call | tf_op jit(solution)/shard_map/pallas_call | solution.py:379
  72.4 1.3 %copy.5 = f32[1280]{0:T(1024)} copy(f32[1280]{0:T(1024)} %shard_map.37) | data formatting | bytes 10240

commit v3 on v2

--- a/solution.py
+++ b/solution.py
@@ -28,11 +28,11 @@
 STRIP = 352
 LAG = 3
 ORDER = [
-    "P0", "S0", "F0", "P1", "S1", "P2", "L", "W1", "F1", "W2", "F2", "S2", "M", "P3", "W3",
-    "F3", "W4", "F4", "S3", "O0", "W5", "F5", "W6", "W7", "F6", "O1", "W8", "F7", "A0", "D0",
-    "W9", "F8", "X0", "W10", "W11", "F9", "O2", "W12", "F10", "A1", "D1", "W13", "F11", "X1",
-    "W14", "W15", "F12", "O3", "O4", "F13", "A2", "D2", "U0", "F14", "X2", "U1", "U2", "F15",
-    "A3", "U3", "D3", "X3", "A4", "U4", "D4", "X4",
+    "F0", "P0", "S0", "N", "P1", "S1", "I", "P2", "W1", "F1", "W2", "F2", "S2", "L", "P3", "W3",
+    "F3", "W4", "F4", "S3", "W5", "F5", "M", "O0", "W6", "W7", "F6", "O1", "W8", "F7", "A0",
+    "D0", "W9", "F8", "X0", "W10", "W11", "F9", "O2", "W12", "F10", "A1", "D1", "W13", "F11",
+    "X1", "W14", "W15", "F12", "O3", "O4", "F13", "A2", "D2", "U0", "F14", "X2", "U1", "U2",
+    "F15", "A3", "U3", "D3", "X3", "A4", "U4", "D4", "X4",
 ]
 
 
@@ -152,12 +152,15 @@
         msend[j] = labels[j:j + 1, :]
     meta[0, 0] = msend[0]
 
+    def sort_group(g):
+        lo, hi = GROUPS[g]
+        take = onehot(iota(((hi - lo) * SHARE, ROWS), 0) + lo * SHARE == slot)
+        outbox[block(lo, hi - lo), :] = dot(take, unit[...]).astype(BF16)
+        if lo == 0:
+            held[0, place(0), :] = outbox[block(0), :]
+
+    sort_group(0)
     pl.semaphore_wait(barrier, len(peers))
-
-    meta_out = []
-    for j in range(1, N_OWN):
-        meta_out.append(copy(msend.at[j], meta.at[0, j], m_s.at[j], m_r.at[j], (dest[j], t)))
-        meta_out[-1].start()
 
     along, across = {}, {}
     out_copies = {}
@@ -178,12 +181,10 @@
             cp.start()
 
     def prepare(g):
-        lo, hi = GROUPS[g]
-        take = onehot(iota(((hi - lo) * SHARE, ROWS), 0) + lo * SHARE == slot)
-        outbox[block(lo, hi - lo), :] = dot(take, unit[...]).astype(BF16)
-        if lo == 0:
-            held[0, place(0), :] = outbox[block(0), :]
+        if g == 0:
             pass_across(0)
+        else:
+            sort_group(g)
 
     def send(g):
         for j in range(max(GROUPS[g][0], 1), GROUPS[g][1]):
@@ -196,23 +197,36 @@
         out_copies[j].wait_recv()
         pass_across(j)
 
-    position = iota((1, TALL), 1)
-    lane_j = jnp.full((1, TALL), -1, jnp.int32)
-    lane_k = jnp.full((1, TALL), -1, jnp.int32)
-    lane_key = jnp.zeros((1, TALL), jnp.int32)
-    for j in range(N_OWN):
-        inside = (position >= PLACE[j]) & (position < PLACE[j] + SHARE)
-        lane_j = jnp.where(inside, j, lane_j)
-        lane_k = jnp.where(inside, position - PLACE[j], lane_k)
-        lane_key = jnp.where(inside, origin[j] * 1024 + position - PLACE[j], lane_key)
-    lane_key = lane_key.astype(F32)
-    tile_of = [t, 2 * y + (1 - k), 2 * down + k, 2 * up + k, 2 * up + (1 - k)]
-    spread = onehot(iota((128, TALL), 0) == lane_k)
-    in_block = onehot(iota((N_OWN, TALL), 0) == lane_j).astype(F32)
-
-    for b in range(5):
-        rowacc[b] = jnp.full((TALL, 128), -1.0, F32)
-        lanebest[b] = jnp.full((1, TALL), -1.0, F32)
+    def find_places():
+        position = iota((1, TALL), 1)
+        lane_j = jnp.full((1, TALL), -1, jnp.int32)
+        lane_k = jnp.full((1, TALL), -1, jnp.int32)
+        lane_key = jnp.zeros((1, TALL), jnp.int32)
+        for j in range(N_OWN):
+            inside = (position >= PLACE[j]) & (position < PLACE[j] + SHARE)
+            lane_j = jnp.where(inside, j, lane_j)
+            lane_k = jnp.where(inside, position - PLACE[j], lane_k)
+            lane_key = jnp.where(inside, origin[j] * 1024 + position - PLACE[j], lane_key)
+        lane_key = lane_key.astype(F32)
+        tile_of = [t, 2 * y + (1 - k), 2 * down + k, 2 * up + k, 2 * up + (1 - k)]
+        spread = onehot(iota((128, TALL), 0) == lane_k)
+        in_block = onehot(iota((N_OWN, TALL), 0) == lane_j).astype(F32)
+        return lane_j, lane_key, tile_of, spread, in_block
+
+    places = []
+
+    def clear():
+        for b in range(5):
+            rowacc[b] = jnp.full((TALL, 128), -1.0, F32)
+            lanebest[b] = jnp.full((1, TALL), -1.0, F32)
+
+    meta_out = []
+
+    def send_labels():
+        for j in range(1, N_OWN):
+            cp = copy(msend.at[j], meta.at[0, j], m_s.at[j], m_r.at[j], (dest[j], t))
+            cp.start()
+            meta_out.append(cp)
 
     meta_fwd = []
 
@@ -224,6 +238,7 @@
             meta_fwd[-1].start()
 
     def take_labels():
+        lane_j, lane_key, tile_of, spread, in_block = places
         for cp in meta_fwd:
             cp.wait()
         for b in range(5):
@@ -293,6 +308,11 @@
             receive(i)
         elif what == "F":
             pass_along(i)
+        elif what == "N":
+            send_labels()
+        elif what == "I":
+            clear()
+            places.extend(find_places())
         elif what == "L":
             pass_labels()
         elif what == "M":
@@ -308,6 +328,7 @@
         else:
             with_far(i)
 
+    spread, in_block = places[3:]
     for b in range(5):
         best = lanebest[b]
         if b != 2:
@@ -319,8 +340,11 @@
     ]
     for cp in back:
         cp.start()
+    left = [cp for j in range(N_OWN - LAG, N_OWN) for cp in along[j]]
+    for cp in [*out_copies.values(), *across.values(), *second.values(), *left]:
+        cp.wait_send()
     for cp in back:
-        cp.wait_recv()
+        cp.wait()
     total = resend[0]
     for b in range(4):
         total = jnp.maximum(total, reget[b])
@@ -331,7 +355,7 @@
     retget[0] = retsend[0]
     returns = [
         copy(retsend.at[j], retget.at[j], t_s.at[j], t_r.at[j], (origin[j], t))
-        for j in range(1, N_OWN)
+        for j in reversed(range(1, N_OWN))
     ]
     for cp in returns:
         cp.start()
@@ -341,8 +365,7 @@
     values = values[:N_OWN] + values[N_OWN:2 * N_OWN] + values[2 * N_OWN:]
     out[...] = jnp.sum(values * own_mask[...], axis=0)
 
-    left = [cp for j in range(N_OWN - LAG, N_OWN) for cp in along[j]]
-    for cp in [*out_copies.values(), *across.values(), *second.values(), *left, *back, *returns]:
+    for cp in returns:
         cp.wait_send()
 
 

time: 73.9 us -> 72.6 us (0.982)
  Pallas kernels: 72.4 us -> 71 us
    pallas_call x1, Pallas kernels: 72.4 us -> 71 us  [on_device(): pl.pallas_call(kernel, out_shape=jax.ShapeDtypeStruct((ROWS,), F32), in_s...]
where the time goes in v3:
time: 72.6 us; the launch traced here: 72.4 us
  Pallas kernels  71 us (98%)
  local copies, waits for them, and re-layouts  1.3 us (2%)
    pallas_call x1, Pallas kernels, on_device(): pl.pallas_call(kernel, out_shape=jax.ShapeDtypeStruct((ROWS,), F32), in_s...  71 us

profile of v3, /device:TPU:1, one launch (start us, length us, event | category | flops | bytes accessed | tf_op | source)
XLA Modules:
  0.0 72.4 jit_solution(3697829279611975933)
XLA Ops:
  0.0 71.0 %shard_map.37 = f32[1280]{0:T(1024)} custom-call(bf16[1280,768]{1,0:T(8,128)(2,1)} %emb_hbm.1, s32[1280]{0:T(1024)} %clu.1, s32[128]{0:T(128)} %omap.1), custom_call_target="tpu_custom_call" | custom-call | tf_op jit(solution)/shard_map/pallas_call | solution.py:402
  71.1 1.3 %copy.5 = f32[1280]{0:T(1024)} copy(f32[1280]{0:T(1024)} %shard_map.37) | data formatting | bytes 10240

commit v4 on v3

--- a/solution.py
+++ b/solution.py
@@ -26,13 +26,13 @@
 GROUPS = [(0, 5), (5, 9), (9, 13), (13, 16)]
 STAGES = [(0, 4), (4, 7), (7, 10), (10, 13), (13, 16)]
 STRIP = 352
-LAG = 3
+LAG = 4
 ORDER = [
     "F0", "P0", "S0", "N", "P1", "S1", "I", "P2", "W1", "F1", "W2", "F2", "S2", "L", "P3", "W3",
     "F3", "W4", "F4", "S3", "W5", "F5", "M", "O0", "W6", "W7", "F6", "O1", "W8", "F7", "A0",
     "D0", "W9", "F8", "X0", "W10", "W11", "F9", "O2", "W12", "F10", "A1", "D1", "W13", "F11",
-    "X1", "W14", "W15", "F12", "O3", "O4", "F13", "A2", "D2", "U0", "F14", "X2", "U1", "U2",
-    "F15", "A3", "U3", "D3", "X3", "A4", "U4", "D4", "X4",
+    "X1", "W14", "W15", "F12", "O3", "O4", "F13", "A2", "D2", "U0", "F14", "X2", "U1", "F15",
+    "U2", "A3", "D3", "U3", "X3", "A4", "D4", "U4", "X4",
 ]
 
 
@@ -253,13 +253,13 @@
 
     second = {}
 
-    def compare(a, b, s, rows):
+    def compare(a, b, s, rows, first=0):
         width = STARTS[s + 1] - STARTS[s]
         new = pl.ds(STARTS[s], width)
         col_clu = lane_clu[a, :, new]
         col_key = lane_keys[a, :, new]
         best = lanebest[a, :, new]
-        for top in range(0, rows, STRIP):
+        for top in range(first, rows, STRIP):
             strip = pl.ds(top, min(STRIP, rows - top))
             scores = dot_t(held[b, strip, :], held[a, new, :])
             same = jnp.where(col_info[b, strip, 0:1] == col_clu, scores, F32(-1.0))
@@ -287,8 +287,10 @@
             second[j].start()
 
     def with_owners(s):
-        compare(3, 0, s, TALL)
-        compare(3, 1, s, TALL)
+        for b in (0, 1):
+            compare(3, b, s, TALL, STARTS[s])
+        for b in (0, 1):
+            compare(2, b, s, TALL, STARTS[s + 1])
 
     def with_above(s):
         compare(2, 3, s, STARTS[s + 1])

time: 72.6 us -> 71 us (0.978)
  Pallas kernels: 71 us -> 69.5 us
    pallas_call x1, Pallas kernels: 71 us -> 69.5 us  [on_device(): pl.pallas_call(kernel, out_shape=jax.ShapeDtypeStruct((ROWS,), F32), in_s...]
where the time goes in v4:
time: 71 us; the launch traced here: 70.8 us
  Pallas kernels  69.5 us (98%)
  local copies, waits for them, and re-layouts  1.3 us (2%)
    pallas_call x1, Pallas kernels, on_device(): pl.pallas_call(kernel, out_shape=jax.ShapeDtypeStruct((ROWS,), F32), in_s...  69.5 us

profile of v4, /device:TPU:1, one launch (start us, length us, event | category | flops | bytes accessed | tf_op | source)
XLA Modules:
  0.0 70.8 jit_solution(17569521599019056120)
XLA Ops:
  0.0 69.5 %shard_map.37 = f32[1280]{0:T(1024)} custom-call(bf16[1280,768]{1,0:T(8,128)(2,1)} %emb_hbm.1, s32[1280]{0:T(1024)} %clu.1, s32[128]{0:T(128)} %omap.1), custom_call_target="tpu_custom_call" | custom-call | tf_op jit(solution)/shard_map/pallas_call | solution.py:404
  69.5 1.3 %copy.5 = f32[1280]{0:T(1024)} copy(f32[1280]{0:T(1024)} %shard_map.37) | data formatting | bytes 10240
